TPU v7x, 512 devices: a whole 4x8x8 slice. The times are simulated.
512 devices in a mesh: grp: 4 (over x), gx: 16 (over y, core), gy: 8 (over z).
Axes of the slice: x: 4, y: 8, z: 8, core: 2. Of those that a mesh axis runs over, the one named last changes fastest.
Arguments:
- source: float32 [256, 128, 512], P('gx', 'gy', 'grp'), may hold values from -13 to 13
- conductance: float32 [256, 128, 512], P('gx', 'gy', 'grp'), may hold values from 0.2 to 5
- storage: float32 [256, 128, 512], P('gx', 'gy', 'grp'), may hold values from 0.05 to 1
- aggregate_ids: int32 [256, 128, 512], P('gx', 'gy', 'grp'), may hold values from 0 to 511, as said below
- coarse_values: float32 [4096, 64, 256], P(('grp', 'gx', 'gy')), as said below
- coarse_columns: int32 [4096, 4], P(('grp', 'gx', 'gy')), may hold values from 0 to 4095, as said below
Outputs:
- solution: float32 [256, 128, 512], P('gx', 'gy', 'grp')
- coarse_error: float32 [262144], P(('grp', 'gx', 'gy'))
Inputs may be any that keep to these rules, and one draw needn't show every extreme that they name: `aggregate_ids`: on each device, every id names exactly the 64 cells of one aligned 4 x 4 x 4 box of the device's block, and different boxes have different ids. `coarse_columns`: entry 0 of block row b is b itself; every other entry names a block of a device whose gx and gy indices differ from those of row b's device by at most one. `coarse_values`: in every row of the coarse operator the diagonal entry of the first stored block exceeds the sum of the magnitudes of all other stored entries of that row.
All inputs are finite; a program needn't handle non-finite values.
Results may differ from a plain program's by a relative error of at most 0.0001.
Values sent between devices are 32-bit elements; how exact they have to be, the bound alone decides.
A program may use at most 64 MiB of HBM per device.

v0:
```python
import jax
import jax.numpy as jnp
from jax import lax
from jax.sharding import PartitionSpec as P

NU = 2
CITER = 4


WEIGHT = 2.0 / 3.0
PAIRS = ((0, 1), (0, -1), (1, 1), (1, -1), (2, 1), (2, -1))


def padded_2(cells, sides, width):
    for axis, dim in sides:
        count = lax.axis_size(axis)
        ends = count - 1
        head = lax.slice_in_dim(cells, 0, width, axis=dim)
        tail = lax.slice_in_dim(cells, cells.shape[dim] - width, cells.shape[dim], axis=dim)
        cells = jnp.concatenate(
            [
                lax.ppermute(tail, axis, [(i, (i + 1) % count) for i in range(ends)]),
                cells,
                lax.ppermute(head, axis, [((i + 1) % count, i) for i in range(ends)]),
            ],
            axis=dim,
        )
    return cells


def shifted(padded, dimension, offset):
    window = [slice(1, -1), slice(1, -1), slice(1, -1)]
    window[dimension] = slice(1 + offset, padded.shape[dimension] - 1 + offset)
    return padded[tuple(window)]


def trimmed(array):
    return array[1:-1, 1:-1, 1:-1]


def apply_wide(padded_field, storage_part, face_part):
    center = trimmed(padded_field)
    summed = storage_part * center
    for position in range(6):
        dimension, offset = PAIRS[position]
        summed = summed + face_part[position] * (center - shifted(padded_field, dimension, offset))
    return summed


def face_terms(padded_cond):
    center = trimmed(padded_cond)
    return [0.5 * (center + shifted(padded_cond, dimension, offset)) for dimension, offset in PAIRS]


def add_faces(storage_part, face_part):
    running = storage_part
    for position in range(6):
        running = running + face_part[position]
    return running


def local(source, conductance, storage, aggregate_ids, coarse_values, coarse_columns):
    size_x, size_y, size_z = source.shape
    padded_cond = padded_2(conductance, (("grp", 2), ("gx", 0), ("gy", 1)), 1)
    face_list = face_terms(padded_cond)
    diagonal = add_faces(storage, face_list)

    def operate(field):
        padded = padded_2(field, (("grp", 2), ("gx", 0), ("gy", 1)), 1)
        return apply_wide(padded, storage, face_list)

    solution = WEIGHT * source / diagonal
    solution = solution + WEIGHT * (source - operate(solution)) / diagonal
    residual = source - operate(solution)
    smoothed = residual - WEIGHT * operate(residual / diagonal)
    box_labels = aggregate_ids[::4, ::4, ::4].reshape(-1)
    box_totals = (
        smoothed.reshape(size_x // 4, 4, size_y // 4, 4, size_z // 4, 4)
        .sum(axis=(1, 3, 5))
        .reshape(-1)
    )
    coarse_rhs = jnp.zeros(box_totals.shape, source.dtype).at[box_labels].set(box_totals)
    coarse_diag = jnp.diagonal(coarse_values[:, :, :64], axis1=1, axis2=2).reshape(-1)
    coarse_error = coarse_rhs / coarse_diag
    for sweep_number in range(CITER - 1):
        gathered = lax.all_gather(coarse_error, ("grp", "gx", "gy"), axis=0, tiled=True)
        blocks = gathered.reshape(-1, 64)[coarse_columns]
        blocks = blocks.reshape(blocks.shape[0], -1)
        applied = jnp.einsum(
            "bim,bm->bi", coarse_values, blocks, precision=lax.Precision.HIGHEST
        ).reshape(-1)
        coarse_error = coarse_error + (coarse_rhs - applied) / coarse_diag
    small_field = coarse_error[box_labels].reshape(size_x // 4, size_y // 4, size_z // 4)
    lifted = jnp.repeat(jnp.repeat(jnp.repeat(small_field, 4, axis=0), 4, axis=1), 4, axis=2)
    solution = solution + (lifted - WEIGHT * operate(lifted) / diagonal)
    for sweep_number in range(NU):
        solution = solution + WEIGHT * (source - operate(solution)) / diagonal
    return (solution, coarse_error)


def solution(mesh):
    return jax.shard_map(
        local,
        mesh=mesh,
        in_specs=(
            P("gx", "gy", "grp"),
            P("gx", "gy", "grp"),
            P("gx", "gy", "grp"),
            P("gx", "gy", "grp"),
            P(("grp", "gx", "gy"), None, None),
            P(("grp", "gx", "gy"), None),
        ),
        out_specs=(P("gx", "gy", "grp"), P(("grp", "gx", "gy"))),
        check_vma=False,
    )
```

profile of v0, /device:TPU:288, one launch (start us, length us, event | category | flops | bytes accessed | tf_op | source)
XLA Modules:
  0.0 583.4 jit_solution(13674778865393548589)
XLA Ops:
  8.3 3.5 collective-permute-start
  14.6 4.1 collective-permute-done.1
  23.9 3.8 collective-permute-done.3
  30.7 3.9 collective-permute-start.5
  39.7 3.4 collective-permute-start.6
  45.6 4.4 collective-permute-done.7
  54.4 3.8 collective-permute-done.9
  60.3 3.9 collective-permute-start.11
  73.3 4.4 collective-permute-done.13
  82.2 3.8 collective-permute-done.15
  88.2 3.9 collective-permute-start.17
  100.7 3.6 collective-permute-done.19
  108.7 3.8 collective-permute-done.21
  114.6 3.9 collective-permute-start.23
  122.8 5.7 reshape.84
  134.6 107.4 %all-gather.7.cloned.1.call-done = f32[512,1,512]{2,1,0:T(1,128)} async-done(((f32[1,1,512]{2,1,0:T(1,128)}), f32[512,1,512]{2,1,0:T(1,128)}) %all-gather.7.cloned.1.call-update) | async-done | bytes 1048592 | tf_op jit(solution)/shard_map/all_gather | solution.py:86
  241.9 3.8 reduce
  251.2 109.6 %all-gather.9.cloned.1.call-done = f32[512,1,512]{2,1,0:T(1,128)} async-done(((f32[1,1,512]{2,1,0:T(1,128)}), f32[512,1,512]{2,1,0:T(1,128)}) %all-gather.9.cloned.1.call-update) | async-done | bytes 1048592 | tf_op jit(solution)/shard_map/all_gather | solution.py:86
  360.8 3.8 reduce.1
  369.8 109.8 %all-gather.11.cloned.1.call-done = f32[512,1,512]{2,1,0:T(1,128)} async-done(((f32[1,1,512]{2,1,0:T(1,128)}), f32[512,1,512]{2,1,0:T(1,128)}) %all-gather.11.cloned.1.call-update) | async-done | bytes 1048592 | tf_op jit(solution)/shard_map/all_gather | solution.py:86
  479.7 3.8 reduce.2
  488.1 3.5 gather_fusion.4
  497.2 3.6 collective-permute-done.25
  505.4 3.8 collective-permute-done.27
  509.4 3.9 collective-permute-start.28
  515.3 4.9 collective-permute-done.29
  526.5 4.4 collective-permute-done.31
  535.3 3.8 collective-permute-done.33
  541.3 3.9 collective-permute-start.35
  554.2 4.4 collective-permute-done.37
  563.0 3.8 collective-permute-done.39
  568.9 3.9 collective-permute-start.41
  (156 shorter events, 126.6 us)
Async XLA Ops:
  7.2 234.7 %all-gather.7.cloned.1.call-start = ((), (), s32[]{:S(2)}) async-start(), calls=%async_computation | async-start | bytes 1050624 | tf_op jit(solution)/shard_map/all_gather | solution.py:86
  8.3 6.3 %collective-permute-start = (f32[16,16,1]{2,1,0:T(8,128)S(1)}, f32[16,16,1]{2,1,0:T(8,128)S(1)}, u32[]{:S(2)}, u32[]{:S(2)}) collective-permute-start(f32[16,16,1]{2,1,0:T(8,128)S(1)} %get-tuple-element.55), channel_id=1, source_target_pairs={{0,128},{128,256},{256,384},{1,129},{129,257},{257,385},{2,130},{1... | collective-permute-start | bytes 3080 | tf_op jit(solution)/shard_map/ppermute | solution.py:22
  11.9 6.9 %collective-permute-start.1 = (f32[16,16,1]{2,1,0:T(8,128)S(1)}, f32[16,16,1]{2,1,0:T(8,128)S(1)}, u32[]{:S(2)}, u32[]{:S(2)}) collective-permute-start(f32[16,16,1]{2,1,0:T(8,128)S(1)} %get-tuple-element.56), channel_id=1, source_target_pairs={{128,0},{256,128},{384,256},{129,1},{257,129},{385,257},{130,2},{2... | collective-permute-start | bytes 3080 | tf_op jit(solution)/shard_map/ppermute | solution.py:24
  21.4 6.3 %collective-permute-start.3 = (f32[1,16,130]{2,1,0:T(8,128)S(1)}, f32[1,16,130]{2,1,0:T(8,128)S(1)}, u32[]{:S(2)}, u32[]{:S(2)}) collective-permute-start(f32[1,16,130]{2,1,0:T(8,128)S(1)} %get-tuple-element.43), channel_id=1, source_target_pairs={{0,8},{8,16},{16,24},{24,32},{32,40},{40,48},{48,56},{56,64},{64,7... | collective-permute-start | bytes 24968 | tf_op jit(solution)/shard_map/ppermute | solution.py:22
  28.8 5.9 %collective-permute-start.4 = (f32[18,1,130]{2,1,0:T(1,128)S(1)}, f32[18,1,130]{2,1,0:T(1,128)S(1)}, u32[]{:S(2)}, u32[]{:S(2)}) collective-permute-start(f32[18,1,130]{2,1,0:T(1,128)S(1)} %get-tuple-element.30), channel_id=1, source_target_pairs={{1,0},{2,1},{3,2},{4,3},{5,4},{6,5},{7,6},{9,8},{10,9},{11,10},{12... | collective-permute-start | bytes 28088 | tf_op jit(solution)/shard_map/ppermute | solution.py:24
  30.7 6.9 %collective-permute-start.5 = (f32[18,1,130]{2,1,0:T(1,128)S(1)}, f32[18,1,130]{2,1,0:T(1,128)S(1)}, u32[]{:S(2)}, u32[]{:S(2)}) collective-permute-start(f32[18,1,130]{2,1,0:T(1,128)S(1)} %get-tuple-element.29), channel_id=1, source_target_pairs={{0,1},{1,2},{2,3},{3,4},{4,5},{5,6},{6,7},{8,9},{9,10},{10,11},{11... | collective-permute-start | bytes 28088 | tf_op jit(solution)/shard_map/ppermute | solution.py:22
  39.7 5.9 %collective-permute-start.6 = (f32[16,16,1]{2,1,0:T(8,128)S(1)}, f32[16,16,1]{2,1,0:T(8,128)S(1)}, u32[]{:S(2)}, u32[]{:S(2)}) collective-permute-start(f32[16,16,1]{2,1,0:T(8,128)S(1)} %get-tuple-element.54), channel_id=1, source_target_pairs={{0,128},{128,256},{256,384},{1,129},{129,257},{257,385},{2,130},{1... | collective-permute-start | bytes 3080 | tf_op jit(solution)/shard_map/ppermute | solution.py:22
  43.1 6.9 %collective-permute-start.7 = (f32[16,16,1]{2,1,0:T(8,128)S(1)}, f32[16,16,1]{2,1,0:T(8,128)S(1)}, u32[]{:S(2)}, u32[]{:S(2)}) collective-permute-start(f32[16,16,1]{2,1,0:T(8,128)S(1)} %get-tuple-element.53), channel_id=1, source_target_pairs={{128,0},{256,128},{384,256},{129,1},{257,129},{385,257},{130,2},{2... | collective-permute-start | bytes 3080 | tf_op jit(solution)/shard_map/ppermute | solution.py:24
  52.0 6.3 %collective-permute-start.9 = (f32[1,16,130]{2,1,0:T(8,128)S(1)}, f32[1,16,130]{2,1,0:T(8,128)S(1)}, u32[]{:S(2)}, u32[]{:S(2)}) collective-permute-start(f32[1,16,130]{2,1,0:T(8,128)S(1)} %get-tuple-element.41), channel_id=1, source_target_pairs={{0,8},{8,16},{16,24},{24,32},{32,40},{40,48},{48,56},{56,64},{64,7... | collective-permute-start | bytes 24968 | tf_op jit(solution)/shard_map/ppermute | solution.py:22
  58.4 5.9 %collective-permute-start.10 = (f32[18,1,130]{2,1,0:T(1,128)S(1)}, f32[18,1,130]{2,1,0:T(1,128)S(1)}, u32[]{:S(2)}, u32[]{:S(2)}) collective-permute-start(f32[18,1,130]{2,1,0:T(1,128)S(1)} %get-tuple-element.27), channel_id=1, source_target_pairs={{1,0},{2,1},{3,2},{4,3},{5,4},{6,5},{7,6},{9,8},{10,9},{11,10},{12... | collective-permute-start | bytes 28088 | tf_op jit(solution)/shard_map/ppermute | solution.py:24
  60.3 6.9 %collective-permute-start.11 = (f32[18,1,130]{2,1,0:T(1,128)S(1)}, f32[18,1,130]{2,1,0:T(1,128)S(1)}, u32[]{:S(2)}, u32[]{:S(2)}) collective-permute-start(f32[18,1,130]{2,1,0:T(1,128)S(1)} %get-tuple-element.28), channel_id=1, source_target_pairs={{0,1},{1,2},{2,3},{3,4},{4,5},{5,6},{6,7},{8,9},{9,10},{10,11},{11... | collective-permute-start | bytes 28088 | tf_op jit(solution)/shard_map/ppermute | solution.py:22
  70.8 6.9 %collective-permute-start.13 = (f32[16,16,1]{2,1,0:T(8,128)S(1)}, f32[16,16,1]{2,1,0:T(8,128)S(1)}, u32[]{:S(2)}, u32[]{:S(2)}) collective-permute-start(f32[16,16,1]{2,1,0:T(8,128)S(1)} %get-tuple-element.51), channel_id=1, source_target_pairs={{128,0},{256,128},{384,256},{129,1},{257,129},{385,257},{130,2},{2... | collective-permute-start | bytes 3080 | tf_op jit(solution)/shard_map/ppermute | solution.py:24
  79.8 6.3 %collective-permute-start.15 = (f32[1,16,130]{2,1,0:T(8,128)S(1)}, f32[1,16,130]{2,1,0:T(8,128)S(1)}, u32[]{:S(2)}, u32[]{:S(2)}) collective-permute-start(f32[1,16,130]{2,1,0:T(8,128)S(1)} %get-tuple-element.39), channel_id=1, source_target_pairs={{0,8},{8,16},{16,24},{24,32},{32,40},{40,48},{48,56},{56,64},{64,7... | collective-permute-start | bytes 24968 | tf_op jit(solution)/shard_map/ppermute | solution.py:22
  86.2 5.9 %collective-permute-start.16 = (f32[18,1,130]{2,1,0:T(1,128)S(1)}, f32[18,1,130]{2,1,0:T(1,128)S(1)}, u32[]{:S(2)}, u32[]{:S(2)}) collective-permute-start(f32[18,1,130]{2,1,0:T(1,128)S(1)} %get-tuple-element.25), channel_id=1, source_target_pairs={{1,0},{2,1},{3,2},{4,3},{5,4},{6,5},{7,6},{9,8},{10,9},{11,10},{12... | collective-permute-start | bytes 28088 | tf_op jit(solution)/shard_map/ppermute | solution.py:24
  88.2 6.9 %collective-permute-start.17 = (f32[18,1,130]{2,1,0:T(1,128)S(1)}, f32[18,1,130]{2,1,0:T(1,128)S(1)}, u32[]{:S(2)}, u32[]{:S(2)}) collective-permute-start(f32[18,1,130]{2,1,0:T(1,128)S(1)} %get-tuple-element.26), channel_id=1, source_target_pairs={{0,1},{1,2},{2,3},{3,4},{4,5},{5,6},{6,7},{8,9},{9,10},{10,11},{11... | collective-permute-start | bytes 28088 | tf_op jit(solution)/shard_map/ppermute | solution.py:22
  97.4 6.9 %collective-permute-start.19 = (f32[16,16,1]{2,1,0:T(8,128)S(1)}, f32[16,16,1]{2,1,0:T(8,128)S(1)}, u32[]{:S(2)}, u32[]{:S(2)}) collective-permute-start(f32[16,16,1]{2,1,0:T(8,128)S(1)} %get-tuple-element.49), channel_id=1, source_target_pairs={{128,0},{256,128},{384,256},{129,1},{257,129},{385,257},{130,2},{2... | collective-permute-start | bytes 3080 | tf_op jit(solution)/shard_map/ppermute | solution.py:24
  106.3 6.3 %collective-permute-start.21 = (f32[1,16,130]{2,1,0:T(8,128)S(1)}, f32[1,16,130]{2,1,0:T(8,128)S(1)}, u32[]{:S(2)}, u32[]{:S(2)}) collective-permute-start(f32[1,16,130]{2,1,0:T(8,128)S(1)} %get-tuple-element.37), channel_id=1, source_target_pairs={{0,8},{8,16},{16,24},{24,32},{32,40},{40,48},{48,56},{56,64},{64,7... | collective-permute-start | bytes 24968 | tf_op jit(solution)/shard_map/ppermute | solution.py:22
  112.7 9.5 %collective-permute-start.22 = (f32[18,1,130]{2,1,0:T(1,128)S(1)}, f32[18,1,130]{2,1,0:T(1,128)S(1)}, u32[]{:S(2)}, u32[]{:S(2)}) collective-permute-start(f32[18,1,130]{2,1,0:T(1,128)S(1)} %get-tuple-element.23), channel_id=1, source_target_pairs={{1,0},{2,1},{3,2},{4,3},{5,4},{6,5},{7,6},{9,8},{10,9},{11,10},{12... | collective-permute-start | bytes 28088 | tf_op jit(solution)/shard_map/ppermute | solution.py:24
  114.6 7.6 %collective-permute-start.23 = (f32[18,1,130]{2,1,0:T(1,128)S(1)}, f32[18,1,130]{2,1,0:T(1,128)S(1)}, u32[]{:S(2)}, u32[]{:S(2)}) collective-permute-start(f32[18,1,130]{2,1,0:T(1,128)S(1)} %get-tuple-element.24), channel_id=1, source_target_pairs={{0,1},{1,2},{2,3},{3,4},{4,5},{5,6},{6,7},{8,9},{9,10},{10,11},{11... | collective-permute-start | bytes 28088 | tf_op jit(solution)/shard_map/ppermute | solution.py:22
  134.3 226.5 %all-gather.9.cloned.1.call-start = ((), (), s32[]{:S(2)}) async-start(), calls=%async_computation.1 | async-start | bytes 1050624 | tf_op jit(solution)/shard_map/all_gather | solution.py:86
  251.0 228.7 %all-gather.11.cloned.1.call-start = ((), (), s32[]{:S(2)}) async-start(), calls=%async_computation.2 | async-start | bytes 1050624 | tf_op jit(solution)/shard_map/all_gather | solution.py:86
  503.0 6.3 %collective-permute-start.27 = (f32[1,16,130]{2,1,0:T(8,128)S(1)}, f32[1,16,130]{2,1,0:T(8,128)S(1)}, u32[]{:S(2)}, u32[]{:S(2)}) collective-permute-start(f32[1,16,130]{2,1,0:T(8,128)S(1)} %get-tuple-element.35), channel_id=1, source_target_pairs={{0,8},{8,16},{16,24},{24,32},{32,40},{40,48},{48,56},{56,64},{64,7... | collective-permute-start | bytes 24968 | tf_op jit(solution)/shard_map/ppermute | solution.py:22
  509.4 5.9 %collective-permute-start.28 = (f32[18,1,130]{2,1,0:T(1,128)S(1)}, f32[18,1,130]{2,1,0:T(1,128)S(1)}, u32[]{:S(2)}, u32[]{:S(2)}) collective-permute-start(f32[18,1,130]{2,1,0:T(1,128)S(1)} %get-tuple-element.21), channel_id=1, source_target_pairs={{1,0},{2,1},{3,2},{4,3},{5,4},{6,5},{7,6},{9,8},{10,9},{11,10},{12... | collective-permute-start | bytes 28088 | tf_op jit(solution)/shard_map/ppermute | solution.py:24
  513.3 6.9 %collective-permute-start.29 = (f32[18,1,130]{2,1,0:T(1,128)S(1)}, f32[18,1,130]{2,1,0:T(1,128)S(1)}, u32[]{:S(2)}, u32[]{:S(2)}) collective-permute-start(f32[18,1,130]{2,1,0:T(1,128)S(1)} %get-tuple-element.22), channel_id=1, source_target_pairs={{0,1},{1,2},{2,3},{3,4},{4,5},{5,6},{6,7},{8,9},{9,10},{10,11},{11... | collective-permute-start | bytes 28088 | tf_op jit(solution)/shard_map/ppermute | solution.py:22
  520.6 5.9 %collective-permute-start.30 = (f32[16,16,1]{2,1,0:T(8,128)S(1)}, f32[16,16,1]{2,1,0:T(8,128)S(1)}, u32[]{:S(2)}, u32[]{:S(2)}) collective-permute-start(f32[16,16,1]{2,1,0:T(8,128)S(1)} %get-tuple-element.48), channel_id=1, source_target_pairs={{0,128},{128,256},{256,384},{1,129},{129,257},{257,385},{2,130},{1... | collective-permute-start | bytes 3080 | tf_op jit(solution)/shard_map/ppermute | solution.py:22
  524.0 6.9 %collective-permute-start.31 = (f32[16,16,1]{2,1,0:T(8,128)S(1)}, f32[16,16,1]{2,1,0:T(8,128)S(1)}, u32[]{:S(2)}, u32[]{:S(2)}) collective-permute-start(f32[16,16,1]{2,1,0:T(8,128)S(1)} %get-tuple-element.47), channel_id=1, source_target_pairs={{128,0},{256,128},{384,256},{129,1},{257,129},{385,257},{130,2},{2... | collective-permute-start | bytes 3080 | tf_op jit(solution)/shard_map/ppermute | solution.py:24
  532.9 6.3 %collective-permute-start.33 = (f32[1,16,130]{2,1,0:T(8,128)S(1)}, f32[1,16,130]{2,1,0:T(8,128)S(1)}, u32[]{:S(2)}, u32[]{:S(2)}) collective-permute-start(f32[1,16,130]{2,1,0:T(8,128)S(1)} %get-tuple-element.33), channel_id=1, source_target_pairs={{0,8},{8,16},{16,24},{24,32},{32,40},{40,48},{48,56},{56,64},{64,7... | collective-permute-start | bytes 24968 | tf_op jit(solution)/shard_map/ppermute | solution.py:22
  541.3 6.9 %collective-permute-start.35 = (f32[18,1,130]{2,1,0:T(1,128)S(1)}, f32[18,1,130]{2,1,0:T(1,128)S(1)}, u32[]{:S(2)}, u32[]{:S(2)}) collective-permute-start(f32[18,1,130]{2,1,0:T(1,128)S(1)} %get-tuple-element.20), channel_id=1, source_target_pairs={{0,1},{1,2},{2,3},{3,4},{4,5},{5,6},{6,7},{8,9},{9,10},{10,11},{11... | collective-permute-start | bytes 28088 | tf_op jit(solution)/shard_map/ppermute | solution.py:22
  551.7 6.9 %collective-permute-start.37 = (f32[16,16,1]{2,1,0:T(8,128)S(1)}, f32[16,16,1]{2,1,0:T(8,128)S(1)}, u32[]{:S(2)}, u32[]{:S(2)}) collective-permute-start(f32[16,16,1]{2,1,0:T(8,128)S(1)} %get-tuple-element.45), channel_id=1, source_target_pairs={{128,0},{256,128},{384,256},{129,1},{257,129},{385,257},{130,2},{2... | collective-permute-start | bytes 3080 | tf_op jit(solution)/shard_map/ppermute | solution.py:24
  560.6 6.3 %collective-permute-start.39 = (f32[1,16,130]{2,1,0:T(8,128)S(1)}, f32[1,16,130]{2,1,0:T(8,128)S(1)}, u32[]{:S(2)}, u32[]{:S(2)}) collective-permute-start(f32[1,16,130]{2,1,0:T(8,128)S(1)} %get-tuple-element.31), channel_id=1, source_target_pairs={{0,8},{8,16},{16,24},{24,32},{32,40},{40,48},{48,56},{56,64},{64,7... | collective-permute-start | bytes 24968 | tf_op jit(solution)/shard_map/ppermute | solution.py:22
  567.0 5.9 %collective-permute-start.40 = (f32[18,1,130]{2,1,0:T(1,128)S(1)}, f32[18,1,130]{2,1,0:T(1,128)S(1)}, u32[]{:S(2)}, u32[]{:S(2)}) collective-permute-start(f32[18,1,130]{2,1,0:T(1,128)S(1)} %get-tuple-element.17), channel_id=1, source_target_pairs={{1,0},{2,1},{3,2},{4,3},{5,4},{6,5},{7,6},{9,8},{10,9},{11,10},{12... | collective-permute-start | bytes 28088 | tf_op jit(solution)/shard_map/ppermute | solution.py:24
  568.9 6.9 %collective-permute-start.41 = (f32[18,1,130]{2,1,0:T(1,128)S(1)}, f32[18,1,130]{2,1,0:T(1,128)S(1)}, u32[]{:S(2)}, u32[]{:S(2)}) collective-permute-start(f32[18,1,130]{2,1,0:T(1,128)S(1)} %get-tuple-element.18), channel_id=1, source_target_pairs={{0,1},{1,2},{2,3},{3,4},{4,5},{5,6},{6,7},{8,9},{9,10},{10,11},{11... | collective-permute-start | bytes 28088 | tf_op jit(solution)/shard_map/ppermute | solution.py:22
  (22 other events, 254.8 us)
Sparse Core Ops, SparseCore 0:
  134.4 107.4 all-gather.6
  251.1 109.6 all-gather.8
  370.0 109.6 all-gather.10
where the time goes:
time: 585 us; the launch traced here: 583 us
  waiting for transfers between devices  408 us (70%)
  starting transfers between devices  102 us (17%)
  local copies, waits for them, and re-layouts  32.4 us (6%)
  other arithmetic  24.2 us (4%)
  between operations  14.5 us (2%)
    all_gather x3, waiting for transfers between devices, local(): lax.all_gather(coarse_error, ('grp', 'gx', 'gy'), axis=0, tiled=True)  327 us
    ppermute x21, starting transfers between devices, padded_2(): lax.ppermute(tail, axis, [(i, (i + 1) % count) for i in range(ends)])  64.1 us
    ppermute x21, waiting for transfers between devices, padded_2(): lax.ppermute(tail, axis, [(i, (i + 1) % count) for i in range(ends)])  52.6 us
    ppermute x21, starting transfers between devices, padded_2(): lax.ppermute(head, axis, [((i + 1) % count, i) for i in range(ends)])  38 us
    ppermute x21, waiting for transfers between devices, padded_2(): lax.ppermute(head, axis, [((i + 1) % count, i) for i in range(ends)])  28.8 us
  transfers between devices with their start and end apart: 45, of which 28 were waited for; matrix products, arithmetic and copies ran while one was open for 1% of the time, Pallas kernels for 0%

commit v1 on v0

v1 whole, which is shorter than its diff:
```python
import jax
import jax.numpy as jnp
from jax import lax
from jax.sharding import PartitionSpec as P
import jax.experimental.pallas as pl
import jax.experimental.pallas.tpu as pltpu


F32 = jnp.float32
BF16 = jnp.bfloat16
WEIGHT = 2.0 / 3.0
KEEP = 1.0 / 3.0
NG, NX, NY = 4, 16, 8
MESH = pl.DeviceIdType.MESH
STEPS = (-1, 1)

COARSE = sorted(
    [(g, x, y) for g in range(4) for x in (0, 1, -1) for y in (0, 1, -1) if (g, x, y) != (0, 0, 0)],
    key=lambda d: -(min(d[0], 4 - d[0]) + abs(d[1]) + abs(d[2])),
)


def slot_of(d):
    return (d[0] * 3 + d[1] % 3) * 3 + d[2] % 3


def device(d):
    g, x, y = lax.axis_index("grp"), lax.axis_index("gx"), lax.axis_index("gy")
    return (lax.rem(g + d[0] + NG, NG), lax.rem(x + d[1] + NX, NX), lax.rem(y + d[2] + NY, NY))


def side(step):
    return 0 if step < 0 else 1


def iota(shape, dim):
    return lax.broadcasted_iota(jnp.int32, shape, dim)


def roll(x, shift, axis):
    return pltpu.roll(x, shift, axis)


def arrive(buffer, sem):
    pltpu.make_async_copy(buffer, buffer, sem).wait()


def kernel(
    src, cond, stor, aggr, cval, ccol,
    out, err,
    vC, vS, vB, vA, vV,
    PY8, PY2, PP, PE, PF,
    RXC, RXS, RXB, RY8, RY2, RXY, RP, RF, RE, RK,
    EC, ES, EB, FX, FY, FZ, G, U0, U1, U2, VV, YZ, Q, QE,
    LAB, W, DG, INV, ROWS, PM, GA, EBUF, TS, RB0, RB1, RB2, FF, RLF, RLX, LP,
    lsem, ssem, rsem, cs, cr,
):
    mg, mx, my = lax.axis_index("grp"), lax.axis_index("gx"), lax.axis_index("gy")

    def send(source, target, n, d):
        pltpu.make_async_remote_copy(
            src_ref=source, dst_ref=target, send_sem=ssem.at[n], recv_sem=rsem.at[n],
            device_id=device(d), device_id_type=MESH,
        ).start()

    barrier = pltpu.get_barrier_semaphore()
    for d in COARSE:
        pl.semaphore_signal(barrier, inc=1, device_id=device(d), device_id_type=MESH)
    loads = [(cond, vC), (stor, vS), (src, vB), (cval, vV)]
    loads = [pltpu.make_async_copy(a, b, lsem.at[n]) for n, (a, b) in enumerate(loads)]
    for n in range(4):
        loads.append(pltpu.make_async_copy(aggr.at[4 * n], vA.at[n], lsem.at[4 + n]))
    for copy in loads:
        copy.start()
    for copy in loads[:3]:
        copy.wait()

    PY8[0, :, 0:3, :] = vC[:, 0:3, :]
    PY8[0, :, 3:5, :] = vS[:, 0:2, :]
    PY8[0, :, 5:7, :] = vB[:, 0:2, :]
    PY8[0, :, 7:8, :] = vS[:, 2:3, :]
    PY2[0, :, 0:1, :] = vC[:, 3:4, :]
    PY2[0, :, 1:2, :] = vB[:, 2:3, :]
    PY8[1, :, 0:3, :] = vC[:, 13:16, :]
    PY8[1, :, 3:5, :] = vS[:, 14:16, :]
    PY8[1, :, 5:7, :] = vB[:, 14:16, :]
    PY8[1, :, 7:8, :] = vS[:, 13:14, :]
    PY2[1, :, 0:1, :] = vC[:, 12:13, :]
    PY2[1, :, 1:2, :] = vB[:, 13:14, :]
    lane16 = iota((16, 128), 1)
    packed = [jnp.zeros((16, 128), F32)] * 3
    for x in range(16):
        mine = lane16 // 8 == x
        packed = [jnp.where(mine, roll(v[x], 8 * x + 4, 1), p) for v, p in zip((vC, vS, vB), packed)]
    pc, ps, pb = packed
    PP[0], PP[1], PP[2] = pc, ps, pb
    edge = jnp.where(lane16 < 40, roll(ps, 24, 1), roll(pb, 40, 1))
    edge = jnp.where(lane16 >= 64, roll(pb, 88, 1), edge)
    edge = jnp.where(lane16 >= 88, roll(ps, 104, 1), edge)
    PE[...] = jnp.where((lane16 < 24) | (lane16 >= 104), pc, edge)
    PF[0, 0:3], PF[0, 3:5], PF[0, 5:7] = pc[0:3], ps[0:2], pb[0:2]
    PF[1, 0:3], PF[1, 3:5], PF[1, 5:7] = pc[13:16], ps[14:16], pb[14:16]
    PF[0, 7:8] = pc[0:1]
    PF[1, 7:8] = pc[0:1]

    pl.semaphore_wait(barrier, len(COARSE))
    for b in STEPS:
        send(PY8.at[side(b)], RY8.at[side(b)], 3, (0, 0, b))
        send(PY2.at[side(b)], RY2.at[side(b)], 4, (0, 0, b))
    for a in STEPS:
        for b in STEPS:
            for c in STEPS:
                send(PE.at[pl.ds(8 * side(c), 8)], RK.at[side(a), side(b), side(c)], 9, (a, b, c))
    for a in STEPS:
        send(PP, RP.at[side(a)], 6, (a, 0, 0))
    for b in STEPS:
        s = side(b)
        send(cond.at[pl.ds(12 * s, 4)], RXC.at[s], 0, (0, b, 0))
        send(stor.at[pl.ds(13 * s, 3)], RXS.at[s], 1, (0, b, 0))
        send(src.at[pl.ds(13 * s, 3)], RXB.at[s], 2, (0, b, 0))
    for a in STEPS:
        for b in STEPS:
            send(PE, RE.at[side(a), side(b)], 8, (a, b, 0))
            send(PF.at[side(b)], RF.at[side(a), side(b)], 7, (a, 0, b))
            send(PY8.at[side(b), pl.ds(13 * side(a), 3)], RXY.at[side(a), side(b)], 5, (0, a, b))

    EC[4:20, 4:20, 0:128] = vC[...]
    ES[4:20, 4:20, 0:128] = vS[...]
    EB[4:20, 4:20, 0:128] = vB[...]
    row, lane = iota((24, 256), 0), iota((24, 256), 1)
    inside = ((row >= 4) | (my > 0)) & ((row < 20) | (my < NY - 1))
    inside &= (lane < 128) | ((lane < 132) & (mg < NG - 1)) | ((lane >= 252) & (mg > 0))
    YZ[...] = inside.astype(jnp.int32)
    for copy in loads[3:]:
        copy.wait()
    for r in range(16):
        LAB[r : r + 1, :] = vA[r // 4, 4 * (r % 4) : 4 * (r % 4) + 1, :]

    def invert(r, inv):
        label = LAB[pl.ds(r, 1), :]
        s8, l8 = iota((8, 128), 0), iota((8, 128), 1)
        mine = (label // 128 == s8 % 4) & (l8 % 4 == 0)
        code = jnp.where(mine, jnp.where(s8 < 4, r, l8 // 4), 0).astype(F32).astype(BF16)
        hot = jnp.where(label % 128 == iota((128, 128), 0), 1.0, 0.0).astype(BF16)
        return inv + lax.dot_general(code, hot, (((1,), (1,)), ((), ())), preferred_element_type=F32)

    inv = lax.fori_loop(0, 16, invert, jnp.zeros((8, 128), F32))
    INV[...] = (inv + 0.5).astype(jnp.int32)

    diag_at = iota((64, 128), 0) == iota((64, 128), 1)
    off_at = iota((64, 256), 0) == iota((64, 256), 1)
    lane1 = iota((1, 128), 1)
    for q in range(4):
        two = []
        for b in (2 * q, 2 * q + 1):
            two.append(jnp.sum(jnp.where(diag_at, vV[b, :, 0:128], 0.0), axis=0, keepdims=True))
            block = jnp.where(off_at, 0.0, vV[b])
            high = block.astype(BF16)
            W[64 * b : 64 * b + 64, :] = high
            W[512 + 64 * b : 576 + 64 * b, :] = (block - high.astype(F32)).astype(BF16)
        DG[q : q + 1, :] = jnp.where(lane1 < 64, two[0], roll(two[1], 64, 1))

    def place(r, c):
        k, b = r // 8, r % 8
        column = ccol[b, k]
        owner, block = column >> 3, column & 7
        dg = (mg - (owner >> 7)) & 3
        dx = lax.rem(mx - ((owner >> 3) & 15) + 3, 3)
        dy = lax.rem(my - (owner & 7) + 3, 3)
        ROWS[r] = ((dg * 3 + dx) * 3 + dy) * 4 + (block >> 1)
        PM[pl.ds(r, 1), :] = jnp.full((1, 128), (block + k) & 1, jnp.int32)
        return c

    lax.fori_loop(0, 32, place, 0)

    arrived = (RXC, RXS, RXB, RY8, RY2, RXY, RP, RF, RE, RK)
    for n, buffer in enumerate(arrived):
        arrive(buffer, rsem.at[n])
    fields = (EC, ES, EB)
    EC[20:24, 4:20, 0:128], EC[0:4, 4:20, 0:128] = RXC[0], RXC[1]
    ES[20:23, 4:20, 0:128], ES[1:4, 4:20, 0:128] = RXS[0], RXS[1]
    EB[20:23, 4:20, 0:128], EB[1:4, 4:20, 0:128] = RXB[0], RXB[1]
    EC[4:20, 20:23, 0:128], EC[4:20, 1:4, 0:128] = RY8[0, :, 0:3], RY8[1, :, 0:3]
    EC[4:20, 23:24, 0:128], EC[4:20, 0:1, 0:128] = RY2[0, :, 0:1], RY2[1, :, 0:1]
    ES[4:20, 20:22, 0:128], ES[4:20, 2:4, 0:128] = RY8[0, :, 3:5], RY8[1, :, 3:5]
    ES[4:20, 22:23, 0:128], ES[4:20, 1:2, 0:128] = RY8[0, :, 7:8], RY8[1, :, 7:8]
    EB[4:20, 20:22, 0:128], EB[4:20, 2:4, 0:128] = RY8[0, :, 5:7], RY8[1, :, 5:7]
    EB[4:20, 22:23, 0:128], EB[4:20, 1:2, 0:128] = RY2[0, :, 1:2], RY2[1, :, 1:2]
    for a in (0, 1):
        x0 = 20 - 19 * a
        EC[x0 : x0 + 3, 20:23, 0:128], EC[x0 : x0 + 3, 1:4, 0:128] = RXY[a, 0, :, 0:3], RXY[a, 1, :, 0:3]
        ES[x0 : x0 + 3, 20:22, 0:128], ES[x0 : x0 + 3, 2:4, 0:128] = RXY[a, 0, :, 3:5], RXY[a, 1, :, 3:5]
        EB[x0 : x0 + 3, 20:22, 0:128], EB[x0 : x0 + 3, 2:4, 0:128] = RXY[a, 0, :, 5:7], RXY[a, 1, :, 5:7]
    low = lane16 % 8 < 4
    low8 = low[0:8]
    for n in range(3):
        Q[n, 4:20] = jnp.where(low, RP[1, n], RP[0, n])
    for b in (0, 1):
        rows = jnp.where(low8, RF[1, b], RF[0, b])
        Q[0, (20, 1)[b] : (23, 4)[b]] = rows[0:3]
        Q[1, (20, 2)[b] : (22, 4)[b]] = rows[3:5]
        Q[2, (20, 2)[b] : (22, 4)[b]] = rows[5:7]
    half, half8 = lane16 < 64, lane16[0:8] < 64
    QE[4:20] = jnp.where(low, jnp.where(half, RE[1, 0], RE[1, 1]), jnp.where(half, RE[0, 0], RE[0, 1]))
    for c in (0, 1):
        rows = jnp.where(
            low8, jnp.where(half8, RK[1, 0, c], RK[1, 1, c]), jnp.where(half8, RK[0, 0, c], RK[0, 1, c])
        )
        QE[(20, 1)[c] : (23, 4)[c]] = rows[(0, 5)[c] : (3, 8)[c]]
    for n in range(3):
        line = Q[n]
        for x in range(16):
            fields[n][4 + x, :, 128:256] = roll(line, 124 - 8 * x, 1)
    line = QE[...]
    for p in range(3):
        EC[20 + p, :, 128:256] = roll(line, 124 - 8 * p, 1)
        EC[1 + p, :, 128:256] = roll(line, 20 - 8 * p, 1)
    for p in range(2):
        ES[20 + p, :, 128:256] = roll(line, 100 - 8 * p, 1)
        ES[2 + p, :, 128:256] = roll(line, 36 - 8 * p, 1)
        EB[20 + p, :, 128:256] = roll(line, 84 - 8 * p, 1)
        EB[2 + p, :, 128:256] = roll(line, 52 - 8 * p, 1)

    def planes(first, last, step, body):
        def some(n, c):
            for j in range(step):
                body(first + n * step + j)
            return c

        lax.fori_loop(0, (last - first) // step, some, 0)

    def valid(i):
        x = ((i >= 4) | (mx > 0)) & ((i < 20) | (mx < NX - 1))
        return YZ[...] * x.astype(jnp.int32) > 0

    def faces(i):
        c = jnp.where(valid(i), EC[i], 0.0)
        EC[i] = c
        FY[i] = 0.5 * (c + roll(c, 23, 0))
        FZ[i] = 0.5 * (c + roll(c, 255, 1))

    planes(0, 24, 4, faces)
    FX[0] = 0.5 * (EC[0] + EC[1])

    def diagonal(i):
        fx = 0.5 * (EC[i] + EC[i + 1])
        FX[i] = fx
        fy, fz = FY[i], FZ[i]
        total = ES[i] + fx + FX[i - 1] + fy + roll(fy, 1, 0) + fz + roll(fz, 1, 1)
        g = jnp.where(valid(i), WEIGHT / total, 0.0)
        G[i] = g
        U0[i] = jnp.where(valid(i), g * EB[i], 0.0)

    planes(1, 23, 2, diagonal)

    def around(i, before, u, after):
        fy, fz = FY[i], FZ[i]
        total = FX[i] * after + FX[i - 1] * before
        total += fy * roll(u, 23, 0) + roll(fy * u, 1, 0)
        return total + (fz * roll(u, 255, 1) + roll(fz * u, 1, 1))

    def first(i):
        v = KEEP * EB[i] + around(i, U0[i - 1], U0[i], U0[i + 1])
        VV[i] = v
        U1[i] = G[i] * v

    def second(i):
        v = KEEP * VV[i] + around(i, U1[i - 1], U1[i], U1[i + 1])
        VV[i] = v
        U2[i] = G[i] * v

    planes(2, 22, 4, first)
    planes(3, 21, 3, second)

    def restrict(n, c):
        total = jnp.zeros((24, 256), F32)
        for j in range(4):
            i = 4 + 4 * n + j
            total += KEEP * VV[i] + around(i, U2[i - 1], U2[i], U2[i + 1])
        total = total[:, 0:128]
        total = total + roll(total, 23, 0)
        total = total + roll(total, 22, 0)
        total = total + roll(total, 127, 1)
        TS[n] = total + roll(total, 126, 1)
        return c

    lax.fori_loop(0, 4, restrict, 0)
    inv_row = INV[0:4]
    inv_lane = 4 * INV[4:8]
    rhs = jnp.zeros((4, 128), F32)
    for r in range(16):
        y = 4 + 4 * (r % 4)
        line = jnp.broadcast_to(TS[r // 4, y : y + 1, :], (4, 128))
        rhs = jnp.where(inv_row == r, jnp.take_along_axis(line, inv_lane, axis=1), rhs)
    inverse = 1.0 / DG[...]
    EBUF[0] = rhs * inverse

    first_half = iota((8, 128), 1) < 64
    row8, lane8 = iota((8, 128), 0), iota((8, 128), 1)
    received = (RB0, RB1, RB2)
    for t, RBUF in enumerate(received):
        for d in COARSE:
            pltpu.make_async_remote_copy(
                src_ref=EBUF.at[t], dst_ref=RBUF.at[slot_of(d)], send_sem=cs.at[t], recv_sem=cr.at[t],
                device_id=device(d), device_id_type=MESH,
            ).start()
        RBUF[0] = EBUF[t]
        arrive(RBUF.at[pl.ds(1, 35)], cr.at[t])

        def fetch(r, c, RBUF=RBUF):
            at = ROWS[r]
            GA[pl.ds(r, 1), :] = RBUF[at >> 2, pl.ds(at & 3, 1), :]
            return c

        lax.fori_loop(0, 32, fetch, 0, unroll=True)
        parts = []
        for k in range(4):
            g = GA[8 * k : 8 * k + 8, :]
            parts.append(jnp.where(PM[8 * k : 8 * k + 8, :] > 0, roll(g, 64, 1), g))
        x = jnp.concatenate(
            [jnp.where(first_half, parts[0], parts[1]), jnp.where(first_half, parts[2], parts[3])], axis=1
        )
        high = x.astype(BF16).astype(F32)
        x = jnp.concatenate([high, x - high], axis=0).astype(BF16)
        y = lax.dot_general(x, W[...], (((1,), (1,)), ((), ())), preferred_element_type=F32)
        y = y[0:8, 0:512] + y[8:16, 0:512] + y[0:8, 512:1024]
        for q in range(4):
            mine = row8 == 2 * q + lane8 // 64
            applied = jnp.sum(jnp.where(mine, y[:, 128 * q : 128 * q + 128], 0.0), axis=0, keepdims=True)
            EBUF[t + 1, q : q + 1, :] = (rhs[q : q + 1] - applied) * inverse[q : q + 1]

    error = EBUF[3]
    err[...] = error
    label = LAB[...]
    field = jnp.zeros((16, 128), F32)
    for q in range(4):
        line = jnp.broadcast_to(error[q : q + 1], (16, 128))
        field = jnp.where(label // 128 == q, jnp.take_along_axis(line, label % 128, axis=1), field)
    for n in range(4):
        FF[n] = field[4 * n : 4 * n + 4]
    for a in (-1, 1, 0):
        for b in (-1, 1, 0):
            for c in (-1, 1, 0):
                if b != 0:
                    send(FF.at[3 * side(b)], RLX.at[side(b), a + 1, c + 1], 10, (a, b, c))
                elif a != 0:
                    send(FF, RLF.at[0 if a < 0 else 1, c + 1], 11, (a, 0, c))
                elif c != 0:
                    send(FF, RLF.at[2, side(c)], 12, (0, 0, c))
    arrive(RLX, rsem.at[10])
    arrive(RLF.at[pl.ds(0, 2)], rsem.at[11])
    arrive(RLF.at[2, pl.ds(0, 2)], rsem.at[12])

    low1 = lane1 < 64
    for n in range(6):
        shown = jnp.int32(1)
        if n == 0:
            shown = (mx > 0).astype(jnp.int32)
        if n == 5:
            shown = (mx < NX - 1).astype(jnp.int32)

        def piece(a, c, yb):
            if n in (0, 5):
                return RLX[0 if n == 5 else 1, a + 1, c + 1, yb : yb + 1]
            if a != 0:
                return RLF[0 if a < 0 else 1, c + 1, n - 1, yb : yb + 1]
            if c != 0:
                return RLF[2, side(c), n - 1, yb : yb + 1]
            return FF[n - 1, yb : yb + 1]

        main, halo = [], []
        for yb in range(-1, 5):
            c, y = (1, 3) if yb < 0 else (-1, 0) if yb > 3 else (0, yb)
            main.append(jnp.broadcast_to(piece(0, c, y), (4, 128)))
            halo.append(jnp.broadcast_to(jnp.where(low1, piece(-1, c, y), piece(1, c, y)), (4, 128)))
        plane = jnp.concatenate([jnp.concatenate(main, axis=0), jnp.concatenate(halo, axis=0)], axis=1)
        LP[n] = jnp.where(YZ[...] * shown > 0, plane, 0.0)

    def corrected(i):
        u = LP[i // 4]
        U2[i] = U0[i] + U1[i] + KEEP * u + G[i] * around(i, LP[(i - 1) // 4], u, LP[(i + 1) // 4])

    def post(i):
        u = U2[i]
        VV[i] = KEEP * u + U0[i] + G[i] * around(i, U2[i - 1], u, U2[i + 1])

    def last(i):
        u = VV[i]
        done = KEEP * u + U0[i] + G[i] * around(i, VV[i - 1], u, VV[i + 1])
        out[i - 4] = done[4:20, 0:128]

    planes(2, 22, 4, corrected)
    planes(3, 21, 3, post)
    planes(4, 20, 4, last)

    for n, buffer in enumerate(arrived):
        arrive(buffer, ssem.at[n])
    for t, RBUF in enumerate(received):
        arrive(RBUF.at[pl.ds(1, 35)], cs.at[t])
    arrive(RLX, ssem.at[10])
    arrive(RLF.at[pl.ds(0, 2)], ssem.at[11])
    arrive(RLF.at[2, pl.ds(0, 2)], ssem.at[12])


def local(source, conductance, storage, aggregate_ids, coarse_values, coarse_columns):
    anywhere = pl.BlockSpec(memory_space=pl.ANY)
    vmem = pl.BlockSpec(memory_space=pltpu.VMEM)
    wide = pltpu.VMEM((24, 24, 256), F32)
    scratch = [pltpu.VMEM((16, 16, 128), F32)] * 3
    scratch += [pltpu.VMEM((4, 16, 128), jnp.int32), pltpu.VMEM((8, 64, 256), F32)]
    sizes = [
        (2, 16, 8, 128), (2, 16, 2, 128), (3, 16, 128), (16, 128), (2, 8, 128),
        (2, 4, 16, 128), (2, 3, 16, 128), (2, 3, 16, 128), (2, 16, 8, 128), (2, 16, 2, 128),
        (2, 2, 3, 8, 128), (2, 3, 16, 128), (2, 2, 8, 128), (2, 2, 16, 128), (2, 2, 2, 8, 128),
    ]
    scratch += [pltpu.VMEM(s, F32) for s in sizes]
    scratch += [wide] * 11
    scratch += [pltpu.VMEM((24, 256), jnp.int32), pltpu.VMEM((3, 24, 128), F32), pltpu.VMEM((24, 128), F32)]
    scratch += [
        pltpu.VMEM((16, 128), jnp.int32),
        pltpu.VMEM((1024, 256), BF16),
        pltpu.VMEM((4, 128), F32),
        pltpu.VMEM((8, 128), jnp.int32),
        pltpu.SMEM((32,), jnp.int32),
        pltpu.VMEM((32, 128), jnp.int32),
        pltpu.VMEM((32, 128), F32),
        pltpu.VMEM((4, 4, 128), F32),
        pltpu.VMEM((4, 24, 128), F32),
        pltpu.VMEM((36, 4, 128), F32),
        pltpu.VMEM((36, 4, 128), F32),
        pltpu.VMEM((36, 4, 128), F32),
        pltpu.VMEM((4, 4, 128), F32),
        pltpu.VMEM((3, 3, 4, 4, 128), F32),
        pltpu.VMEM((2, 3, 3, 4, 128), F32),
        pltpu.VMEM((6, 24, 256), F32),
    ]
    scratch += [pltpu.SemaphoreType.DMA((n,)) for n in (8, 13, 13, 3, 3)]
    solution, error = pl.pallas_call(
        kernel,
        out_shape=(jax.ShapeDtypeStruct((16, 16, 128), F32), jax.ShapeDtypeStruct((4, 128), F32)),
        in_specs=[anywhere] * 5 + [pl.BlockSpec(memory_space=pltpu.SMEM)],
        out_specs=(vmem, vmem),
        scratch_shapes=scratch,
        compiler_params=pltpu.CompilerParams(
            collective_id=0, has_side_effects=True, vmem_limit_bytes=40 * 2**20
        ),
    )(source, conductance, storage, aggregate_ids, coarse_values, coarse_columns)
    return solution, error.reshape(512)


def solution(mesh):
    fine = P("gx", "gy", "grp")
    coarse = ("grp", "gx", "gy")
    return jax.shard_map(
        local,
        mesh=mesh,
        in_specs=(fine, fine, fine, fine, P(coarse, None, None), P(coarse, None)),
        out_specs=(fine, P(coarse)),
        check_vma=False,
    )
```

time: 585 us -> 56.1 us (0.10)
  the two profiles are of different devices: /device:TPU:288 before, /device:TPU:1 now
where the time goes in v1:
time: 56.1 us; the launch traced here: 55.8 us
  Pallas kernels  48.5 us (86%)
  local copies, waits for them, and re-layouts  6.65 us (12%)
  between operations  0.64 us (1%)
    pallas_call x1, Pallas kernels, local(): pl.pallas_call(kernel, out_shape=(jax.ShapeDtypeStruct((16, 16, 128), F32...  48.5 us
    unnamed x13, local copies, waits for them, and re-layouts  6.65 us

profile of v1, /device:TPU:1, one launch (start us, length us, event | category | flops | bytes accessed | tf_op | source)
XLA Modules:
  0.0 55.8 jit_solution(7730575951544475284)
XLA Ops:
  0.6 0.8 %copy.8.ccol = s32[8,4]{1,0:T(8,128)S(1)} copy(s32[8,4]{0,1:T(4,128)} %param.11) | data formatting | bytes 256 | tf_op args[5]
  1.4 0.0 copy-start
  1.4 1.0 %copy-done = f32[8,64,256]{2,1,0:T(8,128)S(1)} copy-done((f32[8,64,256]{2,1,0:T(8,128)S(1)}, f32[8,64,256]{2,1,0:T(8,128)}, u32[]{:S(2)}) %copy-start) | copy-done | bytes 524312
  2.4 0.0 copy-start.1
  2.4 0.9 %copy-done.1 = f32[16,16,128]{2,1,0:T(8,128)S(1)} copy-done((f32[16,16,128]{2,1,0:T(8,128)S(1)}, f32[16,16,128]{2,1,0:T(8,128)}, u32[]{:S(2)}) %copy-start.1) | copy-done | bytes 131096
  3.3 0.0 copy-start.2
  3.3 0.9 %copy-done.2 = f32[16,16,128]{2,1,0:T(8,128)S(1)} copy-done((f32[16,16,128]{2,1,0:T(8,128)S(1)}, f32[16,16,128]{2,1,0:T(8,128)}, u32[]{:S(2)}) %copy-start.2) | copy-done | bytes 131096
  4.2 0.0 copy-start.3
  4.2 0.9 %copy-done.3 = f32[16,16,128]{2,1,0:T(8,128)S(1)} copy-done((f32[16,16,128]{2,1,0:T(8,128)S(1)}, f32[16,16,128]{2,1,0:T(8,128)}, u32[]{:S(2)}) %copy-start.3) | copy-done | bytes 131096
  5.1 0.0 copy-start.4
  5.1 0.9 %copy-done.4 = s32[16,16,128]{2,1,0:T(8,128)S(1)} copy-done((s32[16,16,128]{2,1,0:T(8,128)S(1)}, s32[16,16,128]{2,1,0:T(8,128)}, u32[]{:S(2)}) %copy-start.4) | copy-done | bytes 131096
  6.0 48.5 %shard_map.77 = (f32[16,16,128]{2,1,0:T(8,128)S(1)}, f32[4,128]{1,0:T(4,128)S(1)}) custom-call(f32[16,16,128]{2,1,0:T(8,128)S(1)} %copy-done.1, f32[16,16,128]{2,1,0:T(8,128)S(1)} %copy-done.2, f32[16,16,128]{2,1,0:T(8,128)S(1)} %copy-done.3, s32[16,16,128]{2,1,0:T(8,128)S(1)} %copy-done.4, f32[8,64,256]{2,1,0:T(8,128)S(1)} %copy-done, s32[8,4]{1,0:T(8,128)S(1)} %copy.8.ccol), custom_call_target="tpu_custom_call" | custom-call | tf_op jit(solution)/shard_map/pallas_call | solution.py:438
  54.6 0.7 %copy.11 = f32[16,16,128]{2,1,0:T(8,128)} copy(f32[16,16,128]{2,1,0:T(8,128)S(1)} %get-tuple-element.8) | data formatting | bytes 262144
  55.3 0.6 %copy.12 = f32[512]{0:T(512)} copy(f32[512]{0:T(512)S(1)} %bitcast.1) | data formatting | bytes 4096
Async XLA Ops:
  1.4 1.0 %copy-start = (f32[8,64,256]{2,1,0:T(8,128)S(1)}, f32[8,64,256]{2,1,0:T(8,128)}, u32[]{:S(2)}) copy-start(f32[8,64,256]{2,1,0:T(8,128)} %cval.1) | copy-start | bytes 1572868
  2.4 0.9 %copy-start.1 = (f32[16,16,128]{2,1,0:T(8,128)S(1)}, f32[16,16,128]{2,1,0:T(8,128)}, u32[]{:S(2)}) copy-start(f32[16,16,128]{2,1,0:T(8,128)} %src.1) | copy-start | bytes 393220
  3.3 0.9 %copy-start.2 = (f32[16,16,128]{2,1,0:T(8,128)S(1)}, f32[16,16,128]{2,1,0:T(8,128)}, u32[]{:S(2)}) copy-start(f32[16,16,128]{2,1,0:T(8,128)} %cond.1) | copy-start | bytes 393220
  4.2 0.9 %copy-start.3 = (f32[16,16,128]{2,1,0:T(8,128)S(1)}, f32[16,16,128]{2,1,0:T(8,128)}, u32[]{:S(2)}) copy-start(f32[16,16,128]{2,1,0:T(8,128)} %stor.1) | copy-start | bytes 393220
  5.1 0.9 %copy-start.4 = (s32[16,16,128]{2,1,0:T(8,128)S(1)}, s32[16,16,128]{2,1,0:T(8,128)}, u32[]{:S(2)}) copy-start(s32[16,16,128]{2,1,0:T(8,128)} %aggr.1) | copy-start | bytes 393220

commit v2 on v1

--- a/solution.py
+++ b/solution.py
@@ -1,3 +1,5 @@
+import functools
+
 import jax
 import jax.numpy as jnp
 from jax import lax
@@ -14,14 +16,32 @@
 MESH = pl.DeviceIdType.MESH
 STEPS = (-1, 1)
 
-COARSE = sorted(
-    [(g, x, y) for g in range(4) for x in (0, 1, -1) for y in (0, 1, -1) if (g, x, y) != (0, 0, 0)],
-    key=lambda d: -(min(d[0], 4 - d[0]) + abs(d[1]) + abs(d[2])),
-)
-
-
-def slot_of(d):
-    return (d[0] * 3 + d[1] % 3) * 3 + d[2] % 3
+GROUPS = [(-1, -1), (-1, 1), (1, -1), (1, 1), (0, -1), (0, 1), (-1, 0), (1, 0), (0, 0)]
+
+
+def group_of(x, y):
+    return (x % 3) * 3 + y % 3
+
+
+def members(x, y):
+    return [g for g in (2, 1, 3, 0) if (g, x, y) != (0, 0, 0)]
+
+
+def exists(d):
+    place = (lax.axis_index("grp"), lax.axis_index("gx"), lax.axis_index("gy"))
+    found = None
+    for at, step, count in zip(place, d, (NG, NX, NY)):
+        if step:
+            here = at > 0 if step < 0 else at < count - 1
+            found = here if found is None else found & here
+    return found
+
+
+def when(condition, body):
+    if condition is None:
+        body()
+    else:
+        pl.when(condition)(body)
 
 
 def device(d):
@@ -46,9 +66,9 @@
 
 
 def kernel(
-    src, cond, stor, aggr, cval, ccol,
+    src, cond, stor, aggr, cval, columns,
     out, err,
-    vC, vS, vB, vA, vV,
+    vC, vS, vB, vA, vV, ccol,
     PY8, PY2, PP, PE, PF,
     RXC, RXS, RXB, RY8, RY2, RXY, RP, RF, RE, RK,
     EC, ES, EB, FX, FY, FZ, G, U0, U1, U2, VV, YZ, Q, QE,
@@ -57,21 +77,51 @@
 ):
     mg, mx, my = lax.axis_index("grp"), lax.axis_index("gx"), lax.axis_index("gy")
 
-    def send(source, target, n, d):
-        pltpu.make_async_remote_copy(
-            src_ref=source, dst_ref=target, send_sem=ssem.at[n], recv_sem=rsem.at[n],
-            device_id=device(d), device_id_type=MESH,
-        ).start()
-
-    barrier = pltpu.get_barrier_semaphore()
-    for d in COARSE:
-        pl.semaphore_signal(barrier, inc=1, device_id=device(d), device_id_type=MESH)
-    loads = [(cond, vC), (stor, vS), (src, vB), (cval, vV)]
+    def exchange(messages, base):
+        by_direction = {}
+        for n, (source, target, d) in enumerate(messages):
+            by_direction.setdefault(d, []).append((source, target, base + n))
+
+        def start(d, items):
+            for source, target, n in items:
+                pltpu.make_async_remote_copy(
+                    src_ref=source, dst_ref=target, send_sem=ssem.at[n], recv_sem=rsem.at[n],
+                    device_id=device(d), device_id_type=MESH,
+                ).start()
+
+        def finish(items, sems):
+            for _, target, n in items:
+                arrive(target, sems.at[n])
+
+        for d, items in by_direction.items():
+            when(exists(d), functools.partial(start, d, items))
+
+        def received():
+            for d, items in by_direction.items():
+                when(exists(tuple(-step for step in d)), functools.partial(finish, items, rsem))
+
+        def sent():
+            for d, items in by_direction.items():
+                when(exists(d), functools.partial(finish, items, ssem))
+
+        return received, sent
+
+    loads = [(cond, vC), (stor, vS), (src, vB), (columns, ccol), (cval, vV)]
     loads = [pltpu.make_async_copy(a, b, lsem.at[n]) for n, (a, b) in enumerate(loads)]
     for n in range(4):
-        loads.append(pltpu.make_async_copy(aggr.at[4 * n], vA.at[n], lsem.at[4 + n]))
+        loads.append(pltpu.make_async_copy(aggr.at[4 * n], vA.at[n], lsem.at[5 + n]))
     for copy in loads:
         copy.start()
+    barrier = pltpu.get_barrier_semaphore()
+
+    def greet(x, y):
+        for g in members(x, y):
+            pl.semaphore_signal(barrier, inc=1, device_id=device((g, x, y)), device_id_type=MESH)
+
+    for x, y in GROUPS:
+        when(exists((0, x, y)), functools.partial(greet, x, y))
+    across = 1 + (mx > 0).astype(jnp.int32) + (mx < NX - 1).astype(jnp.int32)
+    along = 1 + (my > 0).astype(jnp.int32) + (my < NY - 1).astype(jnp.int32)
     for copy in loads[:3]:
         copy.wait()
 
@@ -103,26 +153,30 @@
     PF[0, 7:8] = pc[0:1]
     PF[1, 7:8] = pc[0:1]
 
-    pl.semaphore_wait(barrier, len(COARSE))
+    pl.semaphore_wait(barrier, 4 * across * along - 1)
+    messages = []
     for b in STEPS:
-        send(PY8.at[side(b)], RY8.at[side(b)], 3, (0, 0, b))
-        send(PY2.at[side(b)], RY2.at[side(b)], 4, (0, 0, b))
+        messages.append((PY8.at[side(b)], RY8.at[side(b)], (0, 0, b)))
+        messages.append((PY2.at[side(b)], RY2.at[side(b)], (0, 0, b)))
     for a in STEPS:
         for b in STEPS:
             for c in STEPS:
-                send(PE.at[pl.ds(8 * side(c), 8)], RK.at[side(a), side(b), side(c)], 9, (a, b, c))
-    for a in STEPS:
-        send(PP, RP.at[side(a)], 6, (a, 0, 0))
+                target = RK.at[side(a), side(b), side(c)]
+                messages.append((PE.at[pl.ds(8 * side(c), 8)], target, (a, b, c)))
     for b in STEPS:
         s = side(b)
-        send(cond.at[pl.ds(12 * s, 4)], RXC.at[s], 0, (0, b, 0))
-        send(stor.at[pl.ds(13 * s, 3)], RXS.at[s], 1, (0, b, 0))
-        send(src.at[pl.ds(13 * s, 3)], RXB.at[s], 2, (0, b, 0))
+        messages.append((cond.at[pl.ds(12 * s, 4)], RXC.at[s], (0, b, 0)))
+        messages.append((stor.at[pl.ds(13 * s, 3)], RXS.at[s], (0, b, 0)))
+        messages.append((src.at[pl.ds(13 * s, 3)], RXB.at[s], (0, b, 0)))
     for a in STEPS:
         for b in STEPS:
-            send(PE, RE.at[side(a), side(b)], 8, (a, b, 0))
-            send(PF.at[side(b)], RF.at[side(a), side(b)], 7, (a, 0, b))
-            send(PY8.at[side(b), pl.ds(13 * side(a), 3)], RXY.at[side(a), side(b)], 5, (0, a, b))
+            messages.append((PE, RE.at[side(a), side(b)], (a, b, 0)))
+            messages.append((PF.at[side(b)], RF.at[side(a), side(b)], (a, 0, b)))
+            messages.append((PY8.at[side(b), pl.ds(13 * side(a), 3)], RXY.at[side(a), side(b)], (0, a, b)))
+    for a in STEPS:
+        messages.append((PP, RP.at[side(a)], (a, 0, 0)))
+    fine_messages = len(messages)
+    halo_received, halo_sent = exchange(messages, 0)
 
     EC[4:20, 4:20, 0:128] = vC[...]
     ES[4:20, 4:20, 0:128] = vS[...]
@@ -162,20 +216,18 @@
 
     def place(r, c):
         k, b = r // 8, r % 8
-        column = ccol[b, k]
+        column = ccol[k, b]
         owner, block = column >> 3, column & 7
         dg = (mg - (owner >> 7)) & 3
         dx = lax.rem(mx - ((owner >> 3) & 15) + 3, 3)
         dy = lax.rem(my - (owner & 7) + 3, 3)
-        ROWS[r] = ((dg * 3 + dx) * 3 + dy) * 4 + (block >> 1)
+        ROWS[r] = ((dx * 3 + dy) * 4 + dg) * 4 + (block >> 1)
         PM[pl.ds(r, 1), :] = jnp.full((1, 128), (block + k) & 1, jnp.int32)
         return c
 
     lax.fori_loop(0, 32, place, 0)
 
-    arrived = (RXC, RXS, RXB, RY8, RY2, RXY, RP, RF, RE, RK)
-    for n, buffer in enumerate(arrived):
-        arrive(buffer, rsem.at[n])
+    halo_received()
     fields = (EC, ES, EB)
     EC[20:24, 4:20, 0:128], EC[0:4, 4:20, 0:128] = RXC[0], RXC[1]
     ES[20:23, 4:20, 0:128], ES[1:4, 4:20, 0:128] = RXS[0], RXS[1]
@@ -236,6 +288,7 @@
     def faces(i):
         c = jnp.where(valid(i), EC[i], 0.0)
         EC[i] = c
+        EB[i] = jnp.where(valid(i), EB[i], 0.0)
         FY[i] = 0.5 * (c + roll(c, 23, 0))
         FZ[i] = 0.5 * (c + roll(c, 255, 1))
 
@@ -249,7 +302,7 @@
         total = ES[i] + fx + FX[i - 1] + fy + roll(fy, 1, 0) + fz + roll(fz, 1, 1)
         g = jnp.where(valid(i), WEIGHT / total, 0.0)
         G[i] = g
-        U0[i] = jnp.where(valid(i), g * EB[i], 0.0)
+        U0[i] = g * EB[i]
 
     planes(1, 23, 2, diagonal)
 
@@ -298,14 +351,27 @@
     first_half = iota((8, 128), 1) < 64
     row8, lane8 = iota((8, 128), 0), iota((8, 128), 1)
     received = (RB0, RB1, RB2)
+    departures = []
     for t, RBUF in enumerate(received):
-        for d in COARSE:
-            pltpu.make_async_remote_copy(
-                src_ref=EBUF.at[t], dst_ref=RBUF.at[slot_of(d)], send_sem=cs.at[t], recv_sem=cr.at[t],
-                device_id=device(d), device_id_type=MESH,
-            ).start()
+        def post_group(x, y, RBUF=RBUF, t=t):
+            k = group_of(x, y)
+            for g in members(x, y):
+                pltpu.make_async_remote_copy(
+                    src_ref=EBUF.at[t], dst_ref=RBUF.at[4 * k + g], send_sem=cs.at[t, k], recv_sem=cr.at[t, k],
+                    device_id=device((g, x, y)), device_id_type=MESH,
+                ).start()
+
+        def end_group(x, y, sems, RBUF=RBUF, t=t):
+            k, some = group_of(x, y), members(x, y)
+            arrive(RBUF.at[pl.ds(4 * k + 4 - len(some), len(some))], sems.at[t, k])
+
+        for x, y in GROUPS:
+            when(exists((0, x, y)), functools.partial(post_group, x, y))
         RBUF[0] = EBUF[t]
-        arrive(RBUF.at[pl.ds(1, 35)], cr.at[t])
+        for x, y in GROUPS:
+            when(exists((0, -x, -y)), functools.partial(end_group, x, y, cr))
+        for x, y in GROUPS:
+            departures.append((exists((0, x, y)), functools.partial(end_group, x, y, cs)))
 
         def fetch(r, c, RBUF=RBUF):
             at = ROWS[r]
@@ -338,18 +404,18 @@
         field = jnp.where(label // 128 == q, jnp.take_along_axis(line, label % 128, axis=1), field)
     for n in range(4):
         FF[n] = field[4 * n : 4 * n + 4]
-    for a in (-1, 1, 0):
-        for b in (-1, 1, 0):
+    messages = []
+    for b in (-1, 1, 0):
+        for a in (-1, 1, 0):
             for c in (-1, 1, 0):
                 if b != 0:
-                    send(FF.at[3 * side(b)], RLX.at[side(b), a + 1, c + 1], 10, (a, b, c))
+                    messages.append((FF.at[3 * side(b)], RLX.at[side(b), a + 1, c + 1], (a, b, c)))
                 elif a != 0:
-                    send(FF, RLF.at[0 if a < 0 else 1, c + 1], 11, (a, 0, c))
+                    messages.append((FF, RLF.at[side(a), c + 1], (a, 0, c)))
                 elif c != 0:
-                    send(FF, RLF.at[2, side(c)], 12, (0, 0, c))
-    arrive(RLX, rsem.at[10])
-    arrive(RLF.at[pl.ds(0, 2)], rsem.at[11])
-    arrive(RLF.at[2, pl.ds(0, 2)], rsem.at[12])
+                    messages.append((FF, RLF.at[2, side(c)], (0, 0, c)))
+    lifted_received, lifted_sent = exchange(messages, fine_messages)
+    lifted_received()
 
     low1 = lane1 < 64
     for n in range(6):
@@ -393,21 +459,18 @@
     planes(3, 21, 3, post)
     planes(4, 20, 4, last)
 
-    for n, buffer in enumerate(arrived):
-        arrive(buffer, ssem.at[n])
-    for t, RBUF in enumerate(received):
-        arrive(RBUF.at[pl.ds(1, 35)], cs.at[t])
-    arrive(RLX, ssem.at[10])
-    arrive(RLF.at[pl.ds(0, 2)], ssem.at[11])
-    arrive(RLF.at[2, pl.ds(0, 2)], ssem.at[12])
+    halo_sent()
+    for condition, wait in departures:
+        when(condition, wait)
+    lifted_sent()
 
 
 def local(source, conductance, storage, aggregate_ids, coarse_values, coarse_columns):
-    anywhere = pl.BlockSpec(memory_space=pl.ANY)
+    anywhere = pl.BlockSpec(memory_space=pltpu.HBM)
     vmem = pl.BlockSpec(memory_space=pltpu.VMEM)
     wide = pltpu.VMEM((24, 24, 256), F32)
     scratch = [pltpu.VMEM((16, 16, 128), F32)] * 3
-    scratch += [pltpu.VMEM((4, 16, 128), jnp.int32), pltpu.VMEM((8, 64, 256), F32)]
+    scratch += [pltpu.VMEM((4, 16, 128), jnp.int32), pltpu.VMEM((8, 64, 256), F32), pltpu.SMEM((4, 8), jnp.int32)]
     sizes = [
         (2, 16, 8, 128), (2, 16, 2, 128), (3, 16, 128), (16, 128), (2, 8, 128),
         (2, 4, 16, 128), (2, 3, 16, 128), (2, 3, 16, 128), (2, 16, 8, 128), (2, 16, 2, 128),
@@ -434,17 +497,17 @@
         pltpu.VMEM((2, 3, 3, 4, 128), F32),
         pltpu.VMEM((6, 24, 256), F32),
     ]
-    scratch += [pltpu.SemaphoreType.DMA((n,)) for n in (8, 13, 13, 3, 3)]
+    scratch += [pltpu.SemaphoreType.DMA(s) for s in ((9,), (60,), (60,), (3, 9), (3, 9))]
     solution, error = pl.pallas_call(
         kernel,
         out_shape=(jax.ShapeDtypeStruct((16, 16, 128), F32), jax.ShapeDtypeStruct((4, 128), F32)),
-        in_specs=[anywhere] * 5 + [pl.BlockSpec(memory_space=pltpu.SMEM)],
+        in_specs=[anywhere] * 6,
         out_specs=(vmem, vmem),
         scratch_shapes=scratch,
         compiler_params=pltpu.CompilerParams(
-            collective_id=0, has_side_effects=True, vmem_limit_bytes=40 * 2**20
+            collective_id=0, has_side_effects=True, vmem_limit_bytes=56_400_000
         ),
-    )(source, conductance, storage, aggregate_ids, coarse_values, coarse_columns)
+    )(source, conductance, storage, aggregate_ids, coarse_values, coarse_columns.T)
     return solution, error.reshape(512)
 
 

time: 56.1 us -> 47 us (0.84)
  the two profiles are of different devices: /device:TPU:1 before, /device:TPU:25 now
where the time goes in v2:
time: 47 us; the launch traced here: 46.8 us
  Pallas kernels  44.3 us (94%)
  local copies, waits for them, and re-layouts  1.91 us (4%)
  between operations  0.65 us (1%)
    pallas_call x1, Pallas kernels, local(): pl.pallas_call(kernel, out_shape=(jax.ShapeDtypeStruct((16, 16, 128), F32...  44.3 us
    unnamed x4, local copies, waits for them, and re-layouts  1.91 us

profile of v2, /device:TPU:25, one launch (start us, length us, event | category | flops | bytes accessed | tf_op | source)
XLA Modules:
  0.0 46.8 jit_solution(6196491307308357200)
XLA Ops:
  0.6 0.0 copy-start
  0.6 0.7 %copy-done = s32[8,4]{0,1:T(4,128)S(1)} copy-done((s32[8,4]{0,1:T(4,128)S(1)}, s32[8,4]{0,1:T(4,128)}, u32[]{:S(2)}) %copy-start) | copy-done | bytes 152
  1.3 44.3 %shard_map.77 = (f32[16,16,128]{2,1,0:T(8,128)S(1)}, f32[4,128]{1,0:T(4,128)S(1)}) custom-call(f32[16,16,128]{2,1,0:T(8,128)} %src.1, f32[16,16,128]{2,1,0:T(8,128)} %cond.1, f32[16,16,128]{2,1,0:T(8,128)} %stor.1, s32[16,16,128]{2,1,0:T(8,128)} %aggr.1, f32[8,64,256]{2,1,0:T(8,128)} %cval.1, s32[4,8]{1,0:T(4,128)S(1)} %bitcast.2), custom_call_target="tpu_custom_call" | custom-call | tf_op jit(solution)/shard_map/pallas_call | solution.py:501
  45.6 0.7 %copy.10 = f32[16,16,128]{2,1,0:T(8,128)} copy(f32[16,16,128]{2,1,0:T(8,128)S(1)} %get-tuple-element.8) | data formatting | bytes 262144
  46.3 0.6 %copy.11 = f32[512]{0:T(512)} copy(f32[512]{0:T(512)S(1)} %bitcast.3) | data formatting | bytes 4096
Async XLA Ops:
  0.6 0.7 %copy-start = (s32[8,4]{0,1:T(4,128)S(1)}, s32[8,4]{0,1:T(4,128)}, u32[]{:S(2)}) copy-start(s32[8,4]{0,1:T(4,128)} %param.11) | copy-start | bytes 388

commit v3 on v2

--- a/solution.py
+++ b/solution.py
@@ -279,7 +279,7 @@
                 body(first + n * step + j)
             return c
 
-        lax.fori_loop(0, (last - first) // step, some, 0)
+        lax.fori_loop(0, (last - first) // step, some, 0, unroll=True)
 
     def valid(i):
         x = ((i >= 4) | (mx > 0)) & ((i < 20) | (mx < NX - 1))
@@ -337,7 +337,7 @@
         TS[n] = total + roll(total, 126, 1)
         return c
 
-    lax.fori_loop(0, 4, restrict, 0)
+    lax.fori_loop(0, 4, restrict, 0, unroll=True)
     inv_row = INV[0:4]
     inv_lane = 4 * INV[4:8]
     rhs = jnp.zeros((4, 128), F32)

time: 47 us -> 43.4 us (0.923)
  Pallas kernels: 44.3 us -> 40.6 us
    pallas_call x1, Pallas kernels: 44.3 us -> 40.6 us  [local(): pl.pallas_call(kernel, out_shape=(jax.ShapeDtypeStruct((16, 16, 128), F32...]
where the time goes in v3:
time: 43.4 us; the launch traced here: 43.2 us
  Pallas kernels  40.6 us (94%)
  local copies, waits for them, and re-layouts  1.91 us (4%)
  between operations  0.65 us (1%)
    pallas_call x1, Pallas kernels, local(): pl.pallas_call(kernel, out_shape=(jax.ShapeDtypeStruct((16, 16, 128), F32...  40.6 us
    unnamed x4, local copies, waits for them, and re-layouts  1.91 us

profile of v3, /device:TPU:25, one launch (start us, length us, event | category | flops | bytes accessed | tf_op | source)
XLA Modules:
  0.0 43.2 jit_solution(13929055407201538626)
XLA Ops:
  0.6 0.0 copy-start
  0.6 0.7 %copy-done = s32[8,4]{0,1:T(4,128)S(1)} copy-done((s32[8,4]{0,1:T(4,128)S(1)}, s32[8,4]{0,1:T(4,128)}, u32[]{:S(2)}) %copy-start) | copy-done | bytes 152
  1.3 40.6 %shard_map.77 = (f32[16,16,128]{2,1,0:T(8,128)S(1)}, f32[4,128]{1,0:T(4,128)S(1)}) custom-call(f32[16,16,128]{2,1,0:T(8,128)} %src.1, f32[16,16,128]{2,1,0:T(8,128)} %cond.1, f32[16,16,128]{2,1,0:T(8,128)} %stor.1, s32[16,16,128]{2,1,0:T(8,128)} %aggr.1, f32[8,64,256]{2,1,0:T(8,128)} %cval.1, s32[4,8]{1,0:T(4,128)S(1)} %bitcast.2), custom_call_target="tpu_custom_call" | custom-call | tf_op jit(solution)/shard_map/pallas_call | solution.py:501
  42.0 0.7 %copy.10 = f32[16,16,128]{2,1,0:T(8,128)} copy(f32[16,16,128]{2,1,0:T(8,128)S(1)} %get-tuple-element.8) | data formatting | bytes 262144
  42.6 0.6 %copy.11 = f32[512]{0:T(512)} copy(f32[512]{0:T(512)S(1)} %bitcast.3) | data formatting | bytes 4096
Async XLA Ops:
  0.6 0.7 %copy-start = (s32[8,4]{0,1:T(4,128)S(1)}, s32[8,4]{0,1:T(4,128)}, u32[]{:S(2)}) copy-start(s32[8,4]{0,1:T(4,128)} %param.11) | copy-start | bytes 388
